TPU v7x, 256 devices: a whole 4x4x8 slice. The times are simulated.
256 devices in a mesh: row: 8 (over y, core), col: 32 (over x, z).
Axes of the slice: x: 4, y: 4, z: 8, core: 2. Of those that a mesh axis runs over, the one named last changes fastest.
Arguments:
- amplitudes: float32 [8192, 4096], P('row', 'col'), may hold values from -6 to 6
- integrals: float32 [4096, 16384], P(None, 'col'), may hold values from -0.125 to 0.125
- screen: int32 [32, 128], P(None, 'col'), may hold values 0 or 1
- slab_order: int32 [32], replicated, may hold values from 0 to 31, each once
- weights: float32 [8192, 16384], P('row', 'col'), may hold values from 0.05 to 1
Outputs:
- ladder: float32 [8192, 16384], P('row', 'col')
- energy: float32 [], replicated
Inputs may be any that keep to these rules, and one draw needn't show every extreme that they name: `slab_order`: each of 0 to 31 appears once.
All inputs are finite; a program needn't handle non-finite values. No bound on the sum of `screen` on one device may be relied on, other than what follows from the above.
Results may differ from a plain program's by a relative error of at most 0.00007.
Values sent between devices are 32-bit elements; how exact they have to be, the bound alone decides.
No kernel may reach another device: no remote copies, remote signals or barrier semaphores. Data moves between devices by JAX's collectives and lax.ppermute only.
A program may use at most 128 MiB of HBM per device.

v0:
```python
import jax
import jax.numpy as jnp
from jax import lax
from jax.sharding import PartitionSpec as P


def local(amplitudes, integrals, screen, slab_order, weights):
    ktiles = screen.shape[0]
    ncols = screen.shape[1]
    tile_width = integrals.shape[0] // ktiles
    factor = screen.astype(jnp.float32)[:, None, :, None]
    masked = (integrals.reshape(ktiles, tile_width, ncols, tile_width) * factor).reshape(
        ktiles, tile_width, ncols * tile_width
    )
    placed = jnp.take(masked, slab_order, axis=0).reshape(ktiles * tile_width, ncols * tile_width)
    total = jnp.dot(
        lax.all_gather(amplitudes, "col", axis=1, tiled=True),
        placed,
        precision=lax.Precision.HIGHEST,
        preferred_element_type=jnp.float32,
    )
    ladder = 0.5 * total
    all_cells = amplitudes.shape[0] * lax.axis_size("row") * placed.shape[1] * lax.axis_size("col")
    energy = lax.psum(jnp.sum(weights * ladder * ladder), ("row", "col")) / all_cells
    return (ladder, energy)


def solution(mesh):
    return jax.shard_map(
        local,
        mesh=mesh,
        in_specs=(P("row", "col"), P(None, "col"), P(None, "col"), P(), P("row", "col")),
        out_specs=(P("row", "col"), P()),
        check_vma=False,
    )
```

profile of v0, /device:TPU:1, one launch (start us, length us, event | category | flops | bytes accessed | tf_op | source)
XLA Modules:
  0.0 309.5 jit_solution(12734051913290187608)
XLA Ops:
  7.2 0.0 all-gather.2.cloned.1.call-start
  7.2 0.7 all-gather.2.cloned.1.call-update
  7.9 0.7 convert_element_type.3
  8.6 0.1 copy.7
  8.7 0.1 mul.28
  8.8 1.9 copy.8
  10.7 0.7 compare_select_fusion
  11.4 8.3 %broadcast_multiply_fusion = f32[32,128,512]{2,1,0:T(8,128)} fusion(f32[32,128,512]{2,1,0:T(8,128)} %bitcast.13, f32[32,512]{1,0:T(8,128)S(1)} %bitcast.14), kind=kLoop, calls=%fused_computation.2 | loop fusion | flops 2097152 | bytes 16842752 | tf_op jit(solution)/shard_map/mul | solution.py:12
  19.7 0.0 copy-start
  19.7 7.7 %gather_fusion = f32[32,128,512]{2,1,0:T(8,128)} fusion(f32[32,128,512]{2,1,0:T(8,128)} %broadcast_multiply_fusion, s32[1024]{0:T(1024)S(1)} %pad_clamp_fusion), kind=kCustom, calls=%fused_computation | custom fusion | bytes 16777344 | tf_op jit(solution)/shard_map/jit(_take)/gather | solution.py:15
  27.4 0.0 copy-done
  27.4 0.1 broadcast_bitcast_fusion
  27.4 6.0 %bitcast_select_fusion = f32[4096,512]{1,0:T(8,128)} fusion(f32[32,128,512]{2,1,0:T(8,128)} %gather_fusion, pred[4096]{0:T(1024)(128)(4,1)S(1)} %broadcast_bitcast_fusion), kind=kLoop, calls=%fused_computation.1 | loop fusion | flops 2097152 | bytes 16781312 | tf_op jit(solution)/shard_map/jit(_take)/select_n | solution.py:15
  33.4 129.1 %all-gather.2.cloned.1.call-done = f32[1024,4096]{1,0:T(8,128)} async-done(((f32[1024,128]{1,0:T(8,128)}), f32[1024,4096]{1,0:T(8,128)}) %all-gather.2.cloned.1.call-update) | async-done | bytes 16777232 | tf_op jit(solution)/shard_map/all_gather | solution.py:17
  162.5 58.1 %fusion = (f32[]{:T(128)}, f32[1024,512]{0,1:T(8,128)}) fusion(f32[1024,512]{0,1:T(8,128)S(1)} %copy.8, f32[4096,512]{1,0:T(8,128)} %bitcast_select_fusion, f32[1024,4096]{1,0:T(8,128)} %all-gather.2.cloned.1.call-done), kind=kOutput, calls=%fused_computation.4 | convolution fusion | flops 25771900928 | bytes 29360132 | tf_op jit(solution)/shard_map/dot_general | solution.py:16
  220.6 2.9 copy.9
  223.5 77.4 %psum.7 = f32[]{:T(128)} all-reduce(f32[]{:T(128)} %get-tuple-element.4), channel_id=1, replica_groups=mesh['row'=8,'col'=32] {'row','col'}, use_global_device_ids=true, to_apply=%region_1.2 | all-reduce | flops 1 | bytes 8 | tf_op jit(solution)/shard_map/psum | solution.py:24
  (3 shorter events, 0.0 us)
Async XLA Ops:
  7.2 155.3 %all-gather.2.cloned.1.call-start = ((), (), s32[]{:S(2)}) async-start(), calls=%async_computation | async-start | bytes 17301504 | tf_op jit(solution)/shard_map/all_gather | solution.py:17
  19.7 7.7 %copy-start = (s32[32]{0:T(128)S(1)}, s32[32]{0:T(128)}, u32[]{:S(2)}) copy-start(s32[32]{0:T(128)} %param.8) | copy-start | bytes 388
Sparse Core Ops, SparseCore 0:
  10.5 151.9 all-gather.1
where the time goes:
time: 310 us
  waiting for transfers between devices  130 us (42%)
  blocking collectives  77.4 us (25%)
  matrix products  58.1 us (19%)
  between operations  15.8 us (5%)
  other arithmetic  15.6 us (5%)
  local copies, waits for them, and re-layouts  12.8 us (4%)
    all_gather x1, waiting for transfers between devices, local(): lax.all_gather(amplitudes, 'col', axis=1, tiled=True)  129 us
    psum x1, blocking collectives, local(): lax.psum(jnp.sum(weights * ladder * ladder), ('row', 'col')) / all_cells  77.4 us
    dot_general x1, matrix products, local(): jnp.dot(lax.all_gather(amplitudes, 'col', axis=1, tiled=True), placed, pr...  58.1 us
    mul x1, other arithmetic, local(): integrals.reshape(ktiles, tile_width, ncols, tile_width) * factor  8.28 us
    gather x1, local copies, waits for them, and re-layouts, local(): jnp.take(masked, slab_order, axis=0)  7.68 us
    select_n x2, other arithmetic, local(): jnp.take(masked, slab_order, axis=0)  6.63 us
  transfers between devices with their start and end apart: 1, of which 1 were waited for; matrix products, arithmetic and copies ran while one was open for 8% of the time, Pallas kernels for 0%

commit v1 on v0

--- a/solution.py
+++ b/solution.py
@@ -14,7 +14,9 @@
     )
     placed = jnp.take(masked, slab_order, axis=0).reshape(ktiles * tile_width, ncols * tile_width)
     total = jnp.dot(
-        lax.all_gather(amplitudes, "col", axis=1, tiled=True),
+        jnp.concatenate(
+            lax.all_to_all(jnp.stack([amplitudes] * lax.axis_size("col")), "col", 0, 0), axis=1
+        ),
         placed,
         precision=lax.Precision.HIGHEST,
         preferred_element_type=jnp.float32,

time: 310 us -> 571 us (1.84)
  waiting for transfers between devices: 130 us -> 370 us
  blocking collectives: 77.4 us -> 97.1 us
  between operations: 15.8 us -> 2.47 us
  starting transfers between devices: 0.04 us -> 12.1 us
  local copies, waits for them, and re-layouts: 12.8 us -> 21.3 us
  other arithmetic: 15.6 us -> 8.28 us
    all_to_all x0 -> x1, waiting for transfers between devices: none -> 370 us  [local(): lax.all_to_all(jnp.stack([amplitudes] * lax.axis_size('col')), 'col', 0, 0)]
    all_gather x1 -> x0, waiting for transfers between devices: 129 us -> none  [local(): lax.all_gather(amplitudes, 'col', axis=1, tiled=True)]
    psum x1, blocking collectives: 77.4 us -> 97.1 us  [local(): lax.psum(jnp.sum(weights * ladder * ladder), ('row', 'col')) / all_cells]
    all_to_all x0 -> x1, starting transfers between devices: none -> 12.1 us  [local(): lax.all_to_all(jnp.stack([amplitudes] * lax.axis_size('col')), 'col', 0, 0)]
    another operation x0 -> x1, local copies, waits for them, and re-layouts: none -> 8.64 us  [local(): jnp.stack([amplitudes] * lax.axis_size('col'))]
    select_n x2 -> x1, other arithmetic: 6.63 us -> 0.01 us  [local(): jnp.take(masked, slab_order, axis=0)]
  transfers between devices with their start and end apart: 1 -> 1, of which waited for: 1 -> 1; matrix products, arithmetic and copies ran while one was open for 8% -> 3% of each run, Pallas kernels for 0% -> 0%
where the time goes in v1:
time: 571 us; the launch traced here: 570 us
  waiting for transfers between devices  370 us (65%)
  blocking collectives  97.1 us (17%)
  matrix products  58.4 us (10%)
  local copies, waits for them, and re-layouts  21.3 us (4%)
  starting transfers between devices  12.1 us (2%)
  other arithmetic  8.28 us (1%)
    all_to_all x1, waiting for transfers between devices, local(): lax.all_to_all(jnp.stack([amplitudes] * lax.axis_size('col')), 'col', 0, 0)  370 us
    psum x1, blocking collectives, local(): lax.psum(jnp.sum(weights * ladder * ladder), ('row', 'col')) / all_cells  97.1 us
    dot_general x1, matrix products, local(): jnp.dot(jnp.concatenate(lax.all_to_all(jnp.stack([amplitudes] * lax.axis_...  58.4 us
    all_to_all x1, starting transfers between devices, local(): lax.all_to_all(jnp.stack([amplitudes] * lax.axis_size('col')), 'col', 0, 0)  12.1 us
  transfers between devices with their start and end apart: 1, of which 1 were waited for; matrix products, arithmetic and copies ran while one was open for 3% of the time, Pallas kernels for 0%

profile of v1, /device:TPU:1, one launch (start us, length us, event | category | flops | bytes accessed | tf_op | source)
XLA Modules:
  0.0 570.2 jit_solution(15301573667240513680)
XLA Ops:
  0.6 8.6 %stack.2 = f32[32,1024,128]{2,1,0:T(8,128)} broadcast(f32[1024,128]{1,0:T(8,128)} %param.5), dimensions={1,2} | broadcast | bytes 17301504 | tf_op jit(solution)/shard_map/stack | solution.py:18
  9.3 0.0 copy-start
  9.3 0.0 copy-start.2
  9.3 0.0 copy-start.3
  9.3 12.1 %all-to-all-start = ((f32[32,1024,128]{2,1,0:T(8,128)}), f32[32,1024,128]{2,1,0:T(8,128)}, u32[]{:S(2)}, u32[]{:S(2)}) async-start(f32[32,1024,128]{2,1,0:T(8,128)} %stack.2), calls=%async_computation | async-start | bytes 33554432 | tf_op jit(solution)/shard_map/all_to_all | solution.py:18
  21.4 0.0 copy-done
  21.4 1.8 copy.12
  23.2 0.0 copy-done.2
  23.2 0.1 copy.10
  23.3 0.1 mul.28
  23.4 0.0 copy-done.3
  23.5 8.3 %broadcast_multiply_fusion = f32[32,128,512]{2,1,0:T(8,128)} fusion(f32[32,128,512]{2,1,0:T(8,128)} %bitcast.18, f32[32,512]{1,0:T(8,128)S(1)} %bitcast.19), kind=kLoop, calls=%fused_computation.5 | loop fusion | flops 2097152 | bytes 16842752 | tf_op jit(solution)/shard_map/mul | solution.py:12
  31.7 0.0 copy-start.1
  31.7 7.8 %gather_fusion = f32[32,128,512]{2,1,0:T(8,128)} fusion(f32[32,128,512]{2,1,0:T(8,128)} %broadcast_multiply_fusion, s32[1024]{0:T(1024)S(1)} %pad_clamp_fusion), kind=kCustom, calls=%fused_computation | custom fusion | bytes 16777344 | tf_op jit(solution)/shard_map/jit(_take)/gather | solution.py:15
  39.6 370.4 %all-to-all-done = f32[32,1024,128]{2,1,0:T(8,128)} async-done(((f32[32,1024,128]{2,1,0:T(8,128)}), f32[32,1024,128]{2,1,0:T(8,128)}, u32[]{:S(2)}, u32[]{:S(2)}) %all-to-all-start) | async-done | bytes 16777248 | tf_op jit(solution)/shard_map/all_to_all | solution.py:18
  410.0 0.0 copy-done.1
  410.0 58.4 %fusion.5 = (f32[]{:T(128)}, f32[1024,512]{0,1:T(8,128)}) fusion(f32[1024,512]{0,1:T(8,128)S(1)} %copy-done.1, f32[32,1024,128]{2,1,0:T(8,128)} %all-to-all-done, f32[32,128,512]{2,1,0:T(8,128)} %gather_fusion, pred[32]{0:T(512)(128)(4,1)S(1)} %compare_and_fusion), kind=kOutput, calls=%fused_computation.8 | convolution fusion | flops 25773998080 | bytes 29360164 | tf_op jit(solution)/shard_map/dot_general | solution.py:16
  468.4 2.9 copy.13
  471.3 97.1 %psum.7 = f32[]{:T(128)} all-reduce(f32[]{:T(128)} %get-tuple-element.6), channel_id=1, replica_groups=mesh['row'=8,'col'=32] {'row','col'}, use_global_device_ids=true, to_apply=%region_1.2 | all-reduce | flops 1 | bytes 8 | tf_op jit(solution)/shard_map/psum | solution.py:26
  (5 shorter events, 0.0 us)
Async XLA Ops:
  9.3 12.1 %copy-start = (f32[1024,512]{1,0:T(8,128)S(1)}, f32[1024,512]{1,0:T(8,128)}, u32[]{:S(2)}) copy-start(f32[1024,512]{1,0:T(8,128)} %param.9) | copy-start | bytes 6291460
  9.3 14.0 %copy-start.2 = (s32[32,4]{0,1:T(4,128)S(1)}, s32[32,4]{0,1:T(4,128)}, u32[]{:S(2)}) copy-start(s32[32,4]{0,1:T(4,128)} %param.7) | copy-start | bytes 1540
  9.3 14.2 %copy-start.3 = (s32[32]{0:T(128)S(1)}, s32[32]{0:T(128)}, u32[]{:S(2)}) copy-start(s32[32]{0:T(128)} %param.8) | copy-start | bytes 388
  9.3 400.7 %all-to-all-start = ((f32[32,1024,128]{2,1,0:T(8,128)}), f32[32,1024,128]{2,1,0:T(8,128)}, u32[]{:S(2)}, u32[]{:S(2)}) async-start(f32[32,1024,128]{2,1,0:T(8,128)} %stack.2), calls=%async_computation | async-start | bytes 33554432 | tf_op jit(solution)/shard_map/all_to_all | solution.py:18
  31.7 378.2 %copy-start.1 = (f32[1024,512]{0,1:T(8,128)S(1)}, f32[1024,512]{0,1:T(8,128)}, u32[]{:S(2)}) copy-start(f32[1024,512]{0,1:T(8,128)} %copy.12) | copy-start | bytes 6291460
